TPU v7x, 256 devices: a whole 4x4x8 slice. The times are simulated.
256 devices in a mesh: dp: 64 (over z, y, core), mp: 4 (over x).
Axes of the slice: x: 4, y: 4, z: 8, core: 2. Of those that a mesh axis runs over, the one named last changes fastest.
Arguments:
- tokens: bfloat16 [128, 6656], P('dp', 'mp'), may hold values from -6 to 6
- grad_out: bfloat16 [128, 6656], P('dp', 'mp'), may hold values from -1.5 to 1.5
- gate_src: bfloat16 [10240, 6656], P(('dp', 'mp')), may hold values from -0.078125 to 0.078125
- up_src: bfloat16 [10240, 6656], P(('dp', 'mp')), may hold values from -0.078125 to 0.078125
- down_src: bfloat16 [10240, 6656], P(('dp', 'mp')), may hold values from -0.25 to 0.25
- unit_map: int32 [15360], P(('dp', 'mp')), may hold values from 0 to 10239, as said below
- copy_flag: int32 [15360], P(('dp', 'mp')), may hold values from 0 to 1, as said below
Outputs:
- layer_out: bfloat16 [128, 6656], P('dp', 'mp')
- grad_tokens: bfloat16 [128, 6656], P('dp', 'mp')
- grad_gate: bfloat16 [15360, 6656], P(('dp', 'mp'))
- grad_up: bfloat16 [15360, 6656], P(('dp', 'mp'))
- grad_down: bfloat16 [15360, 6656], P(('dp', 'mp'))
Inputs may be any that keep to these rules, and one draw needn't show every extreme that they name: `unit_map`: the widened unit j lies on the device of flat index j // 60 along dp+mp, and its source unit lies on a device with the same mp index. Every source unit is the source of one or two widened units. For every pair of devices, at most 3 widened units of the one have their source on the other; every device takes exactly 3 from some device and gives exactly 3 to some device. `copy_flag`: A source unit with one widened unit gives it flag 1; of a source's two widened units at least one has flag 1.
All inputs are finite; a program needn't handle non-finite values.
Results may differ from a plain program's by a relative error of at most 0.0049.
Values may be sent and summed in bfloat16 or wider, within the bound.
A program may use at most 128 MiB of HBM per device.

v0:
```python
import jax
import jax.numpy as jnp
from jax import lax
from jax.sharding import PartitionSpec as P


def layer_pass(inputs, cotangent, gate_rows, up_rows, down_rows):
    dims = (((1,), (1,)), ((), ()))
    pre_gate = lax.dot_general(inputs, gate_rows, dims, preferred_element_type=jnp.float32)
    pre_up = lax.dot_general(inputs, up_rows, dims, preferred_element_type=jnp.float32)
    sigma = jax.nn.sigmoid(pre_gate)
    active = pre_gate * sigma
    hidden = (active * pre_up).astype(jnp.bfloat16)
    out_part = jnp.dot(hidden, down_rows, preferred_element_type=jnp.float32)
    grad_hidden = lax.dot_general(cotangent, down_rows, dims, preferred_element_type=jnp.float32)
    grad_pre_gate = (grad_hidden * pre_up * (sigma + active * (1.0 - sigma))).astype(jnp.bfloat16)
    grad_pre_up = (grad_hidden * active).astype(jnp.bfloat16)
    input_part = jnp.dot(grad_pre_gate, gate_rows, preferred_element_type=jnp.float32)
    input_part = input_part + jnp.dot(grad_pre_up, up_rows, preferred_element_type=jnp.float32)
    tdims = (((0,), (0,)), ((), ()))
    gate_grad = lax.dot_general(
        grad_pre_gate, inputs, tdims, preferred_element_type=jnp.float32
    ).astype(jnp.bfloat16)
    up_grad = lax.dot_general(
        grad_pre_up, inputs, tdims, preferred_element_type=jnp.float32
    ).astype(jnp.bfloat16)
    down_grad = lax.dot_general(
        hidden, cotangent, tdims, preferred_element_type=jnp.float32
    ).astype(jnp.bfloat16)
    return (out_part, input_part, gate_grad, up_grad, down_grad)


def per_device(tokens, grad_out, gate_src, up_src, down_src, unit_map, copy_flag):
    n_dp = lax.axis_size("dp")
    n_mp = lax.axis_size("mp")
    src_dev = gate_src.shape[0]
    wide_dev = unit_map.shape[0]
    quant = (wide_dev + 3 * n_dp - 1) // (3 * n_dp)
    slots = 3 * quant
    my_mp = lax.axis_index("mp")
    my_flat = lax.axis_index("dp") * n_mp + my_mp
    unit_code = (unit_map * 2 + copy_flag).reshape(-1, 2)
    packed = unit_code[:, 0] + unit_code[:, 1] * 32768
    full_packed = lax.all_gather(packed, ("dp", "mp"), axis=0, tiled=True)
    lower_half = full_packed % 32768
    upper_half = full_packed // 32768
    full_code = jnp.stack([lower_half, upper_half], axis=1).reshape(-1)
    full_map = full_code // 2
    full_flag = full_code % 2
    share = jax.ops.segment_sum(
        full_flag.astype(jnp.float32), full_map, num_segments=src_dev * n_dp * n_mp
    )
    scale = copy_flag.astype(jnp.float32) / share[unit_map]
    owner_dp = unit_map // src_dev // n_mp
    unit_index = jnp.arange(wide_dev, dtype=jnp.int32)
    same_owner = (owner_dp[:, None] == owner_dp[None, :]) & (
        unit_index[:, None] > unit_index[None, :]
    )
    arrival = jnp.sum(same_owner.astype(jnp.int32), axis=1)
    recv_row = owner_dp * slots + arrival
    requests = lax.dynamic_index_in_dim(
        full_map.reshape(n_dp, n_mp, wide_dev), my_mp, 1, keepdims=False
    )
    owned = requests // src_dev == my_flat
    rank = jnp.cumsum(owned.astype(jnp.int32), axis=1) - 1
    slot_ids = jnp.arange(slots, dtype=jnp.int32)
    placed = owned[:, None, :] & (rank[:, None, :] == slot_ids[None, :, None])
    local = requests - my_flat * src_dev
    send_idx = jnp.sum(jnp.where(placed, local[:, None, :], 0), axis=2).reshape(-1)
    tok_feat, cot_feat = (
        lax.all_gather(tokens, "mp", axis=1, tiled=True),
        lax.all_gather(grad_out, "mp", axis=1, tiled=True),
    )
    inputs, cotangent = (
        lax.all_gather(tok_feat, "dp", axis=0, tiled=True),
        lax.all_gather(cot_feat, "dp", axis=0, tiled=True),
    )
    moved_gate, moved_up, moved_down = (
        lax.all_to_all(gate_src[send_idx], "dp", split_axis=0, concat_axis=0, tiled=True),
        lax.all_to_all(up_src[send_idx], "dp", split_axis=0, concat_axis=0, tiled=True),
        lax.all_to_all(down_src[send_idx], "dp", split_axis=0, concat_axis=0, tiled=True),
    )
    gate_wide = moved_gate[recv_row]
    up_wide = moved_up[recv_row]
    down_wide = (moved_down[recv_row].astype(jnp.float32) * scale[:, None]).astype(jnp.bfloat16)
    out_part, input_part, grad_gate, grad_up, grad_down = layer_pass(
        inputs, cotangent, gate_wide, up_wide, down_wide
    )
    out_cols, input_cols = (
        lax.psum_scatter(out_part, "mp", scatter_dimension=1, tiled=True),
        lax.psum_scatter(input_part, "mp", scatter_dimension=1, tiled=True),
    )
    out_sum, input_sum = (
        lax.psum_scatter(out_cols, "dp", scatter_dimension=0, tiled=True),
        lax.psum_scatter(input_cols, "dp", scatter_dimension=0, tiled=True),
    )
    return (
        out_sum.astype(jnp.bfloat16),
        input_sum.astype(jnp.bfloat16),
        grad_gate,
        grad_up,
        grad_down,
    )


def solution(mesh):
    in_specs = (
        P("dp", "mp"),
        P("dp", "mp"),
        P(("dp", "mp"), None),
        P(("dp", "mp"), None),
        P(("dp", "mp"), None),
        P(("dp", "mp")),
        P(("dp", "mp")),
    )
    out_specs = (
        P("dp", "mp"),
        P("dp", "mp"),
        P(("dp", "mp"), None),
        P(("dp", "mp"), None),
        P(("dp", "mp"), None),
    )
    return jax.shard_map(
        per_device, mesh=mesh, in_specs=in_specs, out_specs=out_specs, check_vma=False
    )
```

profile of v0, /device:TPU:2, one launch (start us, length us, event | category | flops | bytes accessed | tf_op | source)
XLA Modules:
  0.0 798.3 jit_solution(5214602645316661995)
XLA Ops:
  8.5 78.8 %all-reduce = s32[7680]{0:T(1024)S(1)} all-reduce(s32[7680]{0:T(1024)S(1)} %dynamic-update-slice), channel_id=2, replica_groups=mesh['dp'=64,'mp'=4] {'dp','mp'}, use_global_device_ids=true, to_apply=%add | all-reduce | flops 7680 | bytes 61440 | tf_op jit(solution)/shard_map/all_gather | solution.py:44
  87.5 2.5 copy.21
  90.0 2.8 reshape.143
  94.0 2.1 gather_fusion.4
  96.1 4.0 all_to_all.30
  100.1 7.7 all-to-all-start.2
  109.9 4.0 all_to_all.27
  113.9 73.3 %all-to-all-done.2 = bf16[64,3,6656]{2,1,0:T(4,128)(2,1)} async-done(((bf16[64,3,6656]{2,1,0:T(4,128)(2,1)}), bf16[64,3,6656]{2,1,0:T(4,128)(2,1)}, u32[]{:S(2)}, u32[]{:S(2)}) %all-to-all-start.2) | async-done | bytes 2555936 | tf_op jit(solution)/shard_map/all_to_all | solution.py:81
  187.2 5.6 all-to-all-start.1
  192.9 11.4 %all_gather.16 = bf16[2,6656]{1,0:T(2,128)(2,1)} all-gather(bf16[2,1664]{1,0:T(2,128)(2,1)S(1)} %copy-done.8), channel_id=1, replica_groups=mesh['dp'=64,'mp'=4] {'mp'}, dimensions={1}, use_global_device_ids=true | all-gather | bytes 33280 | tf_op jit(solution)/shard_map/all_gather | solution.py:71
  204.4 2.1 gather_fusion
  206.5 4.0 all_to_all.24
  210.5 64.6 %all-to-all-done.1 = bf16[64,3,6656]{2,1,0:T(4,128)(2,1)} async-done(((bf16[64,3,6656]{2,1,0:T(4,128)(2,1)}), bf16[64,3,6656]{2,1,0:T(4,128)(2,1)}, u32[]{:S(2)}, u32[]{:S(2)}) %all-to-all-start.1) | async-done | bytes 2555936 | tf_op jit(solution)/shard_map/all_to_all | solution.py:80
  275.1 5.6 all-to-all-start
  280.8 11.4 %all_gather.18 = bf16[2,6656]{1,0:T(2,128)(2,1)} all-gather(bf16[2,1664]{1,0:T(2,128)(2,1)S(1)} %copy-done.9), channel_id=1, replica_groups=mesh['dp'=64,'mp'=4] {'mp'}, dimensions={1}, use_global_device_ids=true | all-gather | bytes 33280 | tf_op jit(solution)/shard_map/all_gather | solution.py:72
  292.5 3.8 reshape.146
  296.3 5.3 reshape.145
  301.9 80.7 %scatter_custom_fusion = f32[10240]{0:T(1024)S(1)} fusion(s32[15360]{0:T(1024)S(1)} %bitcast.37, f32[15360]{0:T(1024)S(1)} %fusion.3, f32[]{:T(128)} %constant.106.clone.1), kind=kCustom, calls=%fused_computation.55 | custom fusion | flops 15360 | bytes 40964 | tf_op jit(solution)/shard_map/scatter-add | solution.py:50
  383.6 3.9 reshape.219
  387.6 4.7 reshape.221
  392.3 6.9 all_to_all.32
  399.2 4.7 gather_fusion.5
  404.0 6.9 all_to_all.29
  410.9 4.7 gather_fusion.3
  415.6 6.9 all_to_all.26
  422.6 3.8 gather_fusion.1
  431.1 2.3 convolution_add_fusion
  434.5 2.4 fusion
  438.9 2.7 convolution_convert_fusion
  444.2 32.5 %reduce-scatter.5.cloned.1.call-done = f32[128,1664]{1,0:T(8,128)} async-done(((f32[128,6656]{1,0:T(8,128)}), f32[128,1664]{1,0:T(8,128)}) %reduce-scatter.5.cloned.1.call-update) | async-done | bytes 851984 | tf_op jit(solution)/shard_map/reduce_scatter | solution.py:91
  476.7 45.1 %reduce-scatter.3.cloned.1.call-done = f32[128,1664]{1,0:T(8,128)} async-done(((f32[128,6656]{1,0:T(8,128)}), f32[128,1664]{1,0:T(8,128)}) %reduce-scatter.3.cloned.1.call-update) | async-done | bytes 851984 | tf_op jit(solution)/shard_map/reduce_scatter | solution.py:90
  521.8 269.4 %all-reduce.5 = (bf16[128,1664]{1,0:T(8,128)(2,1)S(1)}, bf16[128,1664]{1,0:T(8,128)(2,1)S(1)}) all-reduce(f32[128,1664]{1,0:T(8,128)} %reduce-scatter.3.cloned.1.call-done, f32[128,1664]{1,0:T(8,128)} %reduce-scatter.5.cloned.1.call-done), channel_id=4, replica_groups=mesh['dp'=64,'mp'=4] {'dp'}, use_global_device_ids=true, to_apply=%region_5.6.clone | all-reduce | flops 425984 | bytes 2555904
  (73 shorter events, 16.5 us)
Async XLA Ops:
  7.2 86.8 %copy-start = (bf16[40,6656]{1,0:T(8,128)(2,1)S(1)}, bf16[40,6656]{1,0:T(8,128)(2,1)}, u32[]{:S(2)}) copy-start(bf16[40,6656]{1,0:T(8,128)(2,1)} %param.11) | copy-start | bytes 1597444
  100.1 7.7 copy-start.2
  100.1 87.1 %all-to-all-start.2 = ((bf16[64,3,6656]{2,1,0:T(4,128)(2,1)}), bf16[64,3,6656]{2,1,0:T(4,128)(2,1)}, u32[]{:S(2)}, u32[]{:S(2)}) async-start(bf16[64,3,6656]{2,1,0:T(4,128)(2,1)} %all_to_all.30), calls=%async_computation.2 | async-start | bytes 6815744 | tf_op jit(solution)/shard_map/all_to_all | solution.py:81
  113.9 79.0 %copy-start.8 = (bf16[2,1664]{1,0:T(2,128)(2,1)S(1)}, bf16[2,1664]{1,0:T(2,128)(2,1)}, u32[]{:S(2)}) copy-start(bf16[2,1664]{1,0:T(2,128)(2,1)} %param.7) | copy-start | bytes 19972
  113.9 90.4 %copy-start.3 = (bf16[40,6656]{1,0:T(8,128)(2,1)S(1)}, bf16[40,6656]{1,0:T(8,128)(2,1)}, u32[]{:S(2)}) copy-start(bf16[40,6656]{1,0:T(8,128)(2,1)} %param.9) | copy-start | bytes 1597444
  187.2 87.9 %all-to-all-start.1 = ((bf16[64,3,6656]{2,1,0:T(4,128)(2,1)}), bf16[64,3,6656]{2,1,0:T(4,128)(2,1)}, u32[]{:S(2)}, u32[]{:S(2)}) async-start(bf16[64,3,6656]{2,1,0:T(4,128)(2,1)} %all_to_all.27), calls=%async_computation.1 | async-start | bytes 6815744 | tf_op jit(solution)/shard_map/all_to_all | solution.py:80
  192.8 190.8 %all-gather.6.cloned.1.call-start = ((), (), s32[]{:S(2)}) async-start(), calls=%async_computation.7 | async-start | bytes 1730560 | tf_op jit(solution)/shard_map/all_gather | solution.py:75
  210.5 70.3 %copy-start.9 = (bf16[2,1664]{1,0:T(2,128)(2,1)S(1)}, bf16[2,1664]{1,0:T(2,128)(2,1)}, u32[]{:S(2)}) copy-start(bf16[2,1664]{1,0:T(2,128)(2,1)} %param.8) | copy-start | bytes 19972
  275.1 140.5 %all-to-all-start = ((bf16[64,3,6656]{2,1,0:T(4,128)(2,1)}), bf16[64,3,6656]{2,1,0:T(4,128)(2,1)}, u32[]{:S(2)}, u32[]{:S(2)}) async-start(bf16[64,3,6656]{2,1,0:T(4,128)(2,1)} %all_to_all.24), calls=%async_computation | async-start | bytes 6815744 | tf_op jit(solution)/shard_map/all_to_all | solution.py:79
  280.8 106.8 %all-gather.8.cloned.1.call-start = ((), (), s32[]{:S(2)}) async-start(), calls=%async_computation.8 | async-start | bytes 1730560 | tf_op jit(solution)/shard_map/all_gather | solution.py:76
  292.3 184.4 %reduce-scatter.5.cloned.1.call-start = ((), (), s32[]{:S(2)}) async-start(), calls=%async_computation.6 | async-start | bytes 4259840 | tf_op jit(solution)/shard_map/reduce_scatter | solution.py:91
  296.3 87.3 %copy-start.10 = (s32[60]{0:T(128)S(1)}, s32[60]{0:T(128)}, u32[]{:S(2)}) copy-start(s32[60]{0:T(128)} %param.13) | copy-start | bytes 724
  426.4 2.7 copy-start.4
  426.4 2.7 copy-start.5
  429.9 1.2 copy-start.7
  433.4 1.2 copy-start.6
  433.4 88.4 %reduce-scatter.3.cloned.1.call-start = ((), (), s32[]{:S(2)}) async-start(), calls=%async_computation.5 | async-start | bytes 4259840 | tf_op jit(solution)/shard_map/reduce_scatter | solution.py:90
  437.0 0.7 copy-start.11
  441.6 350.2 %copy-start.1 = (bf16[40,6656]{1,0:T(8,128)(2,1)S(1)}, bf16[40,6656]{1,0:T(8,128)(2,1)}, u32[]{:S(2)}) copy-start(bf16[40,6656]{1,0:T(8,128)(2,1)} %param.11) | copy-start | bytes 1597444
Sparse Core Ops, SparseCore 0:
  204.5 84.0 all-gather.5
  292.4 84.0 all-gather.7
  433.5 43.0 reduce-scatter.4
  479.1 42.6 reduce-scatter.2
where the time goes:
time: 800 us; the launch traced here: 798 us
  blocking collectives  371 us (46%)
  waiting for transfers between devices  216 us (27%)
  other arithmetic  83.1 us (10%)
  local copies, waits for them, and re-layouts  80.3 us (10%)
  starting transfers between devices  19.3 us (2%)
  between operations  14.9 us (2%)
  matrix products  14.1 us (2%)
    unnamed x1, blocking collectives  269 us
    scatter-add x1, other arithmetic, per_device(): jax.ops.segment_sum(full_flag.astype(jnp.float32), full_map, num_segments...  80.7 us
    all_gather x1, blocking collectives, per_device(): full_packed = lax.all_gather(packed, ('dp', 'mp'), axis=0, tiled=True)  78.8 us
    all_to_all x1, waiting for transfers between devices, per_device(): lax.all_to_all(down_src[send_idx], 'dp', split_axis=0, concat_axis=0, til...  73.3 us
    all_to_all x1, waiting for transfers between devices, per_device(): lax.all_to_all(up_src[send_idx], 'dp', split_axis=0, concat_axis=0, tiled...  64.6 us
    reduce_scatter x1, waiting for transfers between devices, per_device(): lax.psum_scatter(out_part, 'mp', scatter_dimension=1, tiled=True)  45.1 us
    reduce_scatter x1, waiting for transfers between devices, per_device(): lax.psum_scatter(input_part, 'mp', scatter_dimension=1, tiled=True)  32.5 us
  transfers between devices with their start and end apart: 7, of which 4 were waited for; matrix products, arithmetic and copies ran while one was open for 15% of the time, Pallas kernels for 0%

commit v1 on v0

--- a/solution.py
+++ b/solution.py
@@ -41,7 +41,10 @@
     my_flat = lax.axis_index("dp") * n_mp + my_mp
     unit_code = (unit_map * 2 + copy_flag).reshape(-1, 2)
     packed = unit_code[:, 0] + unit_code[:, 1] * 32768
-    full_packed = lax.all_gather(packed, ("dp", "mp"), axis=0, tiled=True)
+    devices = lax.axis_size(("dp", "mp"))
+    blocks = jnp.stack([packed for _ in range(devices)])
+    blocks = lax.all_to_all(blocks, ("dp", "mp"), split_axis=0, concat_axis=0)
+    full_packed = jnp.concatenate(blocks, axis=0)
     lower_half = full_packed % 32768
     upper_half = full_packed // 32768
     full_code = jnp.stack([lower_half, upper_half], axis=1).reshape(-1)

time: 800 us -> 748 us (0.935)
  blocking collectives: 371 us -> 295 us
  starting transfers between devices: 19.3 us -> 32.1 us
  waiting for transfers between devices: 216 us -> 225 us
    all_gather x1 -> x0, blocking collectives: 78.8 us -> none  [per_device(): full_packed = lax.all_gather(packed, ('dp', 'mp'), axis=0, tiled=True)]
    all_to_all x0 -> x1, starting transfers between devices: none -> 14.7 us  [per_device(): blocks = lax.all_to_all(blocks, ('dp', 'mp'), split_axis=0, concat_axis=0)]
    all_to_all x0 -> x1, waiting for transfers between devices: none -> 11.3 us  [per_device(): blocks = lax.all_to_all(blocks, ('dp', 'mp'), split_axis=0, concat_axis=0)]
  transfers between devices with their start and end apart: 7 -> 8, of which waited for: 4 -> 5; matrix products, arithmetic and copies ran while one was open for 15% -> 16% of each run, Pallas kernels for 0% -> 0%
where the time goes in v1:
time: 748 us; the launch traced here: 746 us
  blocking collectives  295 us (39%)
  waiting for transfers between devices  225 us (30%)
  other arithmetic  84.2 us (11%)
  local copies, waits for them, and re-layouts  81.2 us (11%)
  starting transfers between devices  32.1 us (4%)
  between operations  14.8 us (2%)
  matrix products  14.1 us (2%)
    unnamed x1, blocking collectives  269 us
    scatter-add x1, other arithmetic, per_device(): jax.ops.segment_sum(full_flag.astype(jnp.float32), full_map, num_segments...  80.7 us
    all_to_all x1, waiting for transfers between devices, per_device(): lax.all_to_all(down_src[send_idx], 'dp', split_axis=0, concat_axis=0, til...  73.3 us
    all_to_all x1, waiting for transfers between devices, per_device(): lax.all_to_all(up_src[send_idx], 'dp', split_axis=0, concat_axis=0, tiled...  62.9 us
    reduce_scatter x1, waiting for transfers between devices, per_device(): lax.psum_scatter(out_part, 'mp', scatter_dimension=1, tiled=True)  45.1 us
    reduce_scatter x1, waiting for transfers between devices, per_device(): lax.psum_scatter(input_part, 'mp', scatter_dimension=1, tiled=True)  32.5 us
  transfers between devices with their start and end apart: 8, of which 5 were waited for; matrix products, arithmetic and copies ran while one was open for 16% of the time, Pallas kernels for 0%

profile of v1, /device:TPU:2, one launch (start us, length us, event | category | flops | bytes accessed | tf_op | source)
XLA Modules:
  0.0 746.2 jit_solution(41496251250129796)
XLA Ops:
  9.0 14.7 %all-to-all-start = ((s32[256,1,30]{2,1,0:T(1,128)}), s32[256,1,30]{2,1,0:T(1,128)S(1)}, u32[]{:S(2)}, u32[]{:S(2)}) async-start(s32[256,1,30]{2,1,0:T(1,128)} %stack.4), calls=%async_computation | async-start | bytes 262144 | tf_op jit(solution)/shard_map/all_to_all | solution.py:46
  23.7 11.3 %all-to-all-done = s32[256,1,30]{2,1,0:T(1,128)S(1)} async-done(((s32[256,1,30]{2,1,0:T(1,128)}), s32[256,1,30]{2,1,0:T(1,128)S(1)}, u32[]{:S(2)}, u32[]{:S(2)}) %all-to-all-start) | async-done | bytes 30752 | tf_op jit(solution)/shard_map/all_to_all | solution.py:46
  36.9 2.5 copy.21
  39.4 2.8 reshape.260
  43.4 2.1 gather_fusion.4
  45.5 4.0 all_to_all.35
  49.5 5.7 all-to-all-start.3
  57.3 4.0 all_to_all.32
  61.3 73.3 %all-to-all-done.3 = bf16[64,3,6656]{2,1,0:T(4,128)(2,1)} async-done(((bf16[64,3,6656]{2,1,0:T(4,128)(2,1)}), bf16[64,3,6656]{2,1,0:T(4,128)(2,1)}, u32[]{:S(2)}, u32[]{:S(2)}) %all-to-all-start.3) | async-done | bytes 2555936 | tf_op jit(solution)/shard_map/all_to_all | solution.py:84
  134.6 5.6 all-to-all-start.2
  140.3 12.6 %all_gather.12 = bf16[2,6656]{1,0:T(2,128)(2,1)} all-gather(bf16[2,1664]{1,0:T(2,128)(2,1)S(1)} %copy-done.8), channel_id=1, replica_groups=mesh['dp'=64,'mp'=4] {'mp'}, dimensions={1}, use_global_device_ids=true | all-gather | bytes 33280 | tf_op jit(solution)/shard_map/all_gather | solution.py:74
  155.0 4.0 all_to_all.29
  159.0 62.9 %all-to-all-done.2 = bf16[64,3,6656]{2,1,0:T(4,128)(2,1)} async-done(((bf16[64,3,6656]{2,1,0:T(4,128)(2,1)}), bf16[64,3,6656]{2,1,0:T(4,128)(2,1)}, u32[]{:S(2)}, u32[]{:S(2)}) %all-to-all-start.2) | async-done | bytes 2555936 | tf_op jit(solution)/shard_map/all_to_all | solution.py:83
  221.9 5.9 all-to-all-start.1
  227.9 12.5 %all_gather.14 = bf16[2,6656]{1,0:T(2,128)(2,1)} all-gather(bf16[2,1664]{1,0:T(2,128)(2,1)S(1)} %copy-done.9), channel_id=1, replica_groups=mesh['dp'=64,'mp'=4] {'mp'}, dimensions={1}, use_global_device_ids=true | all-gather | bytes 33280 | tf_op jit(solution)/shard_map/all_gather | solution.py:75
  240.7 3.8 reshape.263
  244.5 5.3 reshape.262
  250.1 80.7 %scatter_custom_fusion = f32[10240]{0:T(1024)S(1)} fusion(s32[15360]{0:T(1024)S(1)} %bitcast.37, f32[15360]{0:T(1024)S(1)} %fusion.3, f32[]{:T(128)} %constant.106.clone.1), kind=kCustom, calls=%fused_computation.52 | custom fusion | flops 15360 | bytes 40964 | tf_op jit(solution)/shard_map/scatter-add | solution.py:53
  331.6 3.9 reshape.333
  335.5 4.7 reshape.335
  340.3 6.9 all_to_all.37
  347.2 4.7 gather_fusion.5
  351.9 6.9 all_to_all.34
  358.8 4.7 gather_fusion.3
  363.6 6.9 all_to_all.31
  370.5 3.8 gather_fusion.1
  379.0 2.3 convolution_add_fusion
  382.5 2.4 fusion
  386.8 2.7 convolution_convert_fusion
  392.1 32.5 %reduce-scatter.5.cloned.1.call-done = f32[128,1664]{1,0:T(8,128)} async-done(((f32[128,6656]{1,0:T(8,128)}), f32[128,1664]{1,0:T(8,128)}) %reduce-scatter.5.cloned.1.call-update) | async-done | bytes 851984 | tf_op jit(solution)/shard_map/reduce_scatter | solution.py:94
  424.6 45.1 %reduce-scatter.3.cloned.1.call-done = f32[128,1664]{1,0:T(8,128)} async-done(((f32[128,6656]{1,0:T(8,128)}), f32[128,1664]{1,0:T(8,128)}) %reduce-scatter.3.cloned.1.call-update) | async-done | bytes 851984 | tf_op jit(solution)/shard_map/reduce_scatter | solution.py:93
  469.7 269.3 %all-reduce.4 = (bf16[128,1664]{1,0:T(8,128)(2,1)S(1)}, bf16[128,1664]{1,0:T(8,128)(2,1)S(1)}) all-reduce(f32[128,1664]{1,0:T(8,128)} %reduce-scatter.3.cloned.1.call-done, f32[128,1664]{1,0:T(8,128)} %reduce-scatter.5.cloned.1.call-done), channel_id=3, replica_groups=mesh['dp'=64,'mp'=4] {'dp'}, use_global_device_ids=true, to_apply=%region_5.6.clone | all-reduce | flops 425984 | bytes 2555904
  (75 shorter events, 20.6 us)
Async XLA Ops:
  7.2 36.3 %copy-start = (bf16[40,6656]{1,0:T(8,128)(2,1)S(1)}, bf16[40,6656]{1,0:T(8,128)(2,1)}, u32[]{:S(2)}) copy-start(bf16[40,6656]{1,0:T(8,128)(2,1)} %param.11) | copy-start | bytes 1597444
  9.0 26.0 %all-to-all-start = ((s32[256,1,30]{2,1,0:T(1,128)}), s32[256,1,30]{2,1,0:T(1,128)S(1)}, u32[]{:S(2)}, u32[]{:S(2)}) async-start(s32[256,1,30]{2,1,0:T(1,128)} %stack.4), calls=%async_computation | async-start | bytes 262144 | tf_op jit(solution)/shard_map/all_to_all | solution.py:46
  49.5 5.7 copy-start.2
  49.5 85.1 %all-to-all-start.3 = ((bf16[64,3,6656]{2,1,0:T(4,128)(2,1)}), bf16[64,3,6656]{2,1,0:T(4,128)(2,1)}, u32[]{:S(2)}, u32[]{:S(2)}) async-start(bf16[64,3,6656]{2,1,0:T(4,128)(2,1)} %all_to_all.35), calls=%async_computation.3 | async-start | bytes 6815744 | tf_op jit(solution)/shard_map/all_to_all | solution.py:84
  61.3 79.0 %copy-start.8 = (bf16[2,1664]{1,0:T(2,128)(2,1)S(1)}, bf16[2,1664]{1,0:T(2,128)(2,1)}, u32[]{:S(2)}) copy-start(bf16[2,1664]{1,0:T(2,128)(2,1)} %param.7) | copy-start | bytes 19972
  61.3 91.6 %copy-start.3 = (bf16[40,6656]{1,0:T(8,128)(2,1)S(1)}, bf16[40,6656]{1,0:T(8,128)(2,1)}, u32[]{:S(2)}) copy-start(bf16[40,6656]{1,0:T(8,128)(2,1)} %param.9) | copy-start | bytes 1597444
  134.6 87.2 %all-to-all-start.2 = ((bf16[64,3,6656]{2,1,0:T(4,128)(2,1)}), bf16[64,3,6656]{2,1,0:T(4,128)(2,1)}, u32[]{:S(2)}, u32[]{:S(2)}) async-start(bf16[64,3,6656]{2,1,0:T(4,128)(2,1)} %all_to_all.32), calls=%async_computation.2 | async-start | bytes 6815744 | tf_op jit(solution)/shard_map/all_to_all | solution.py:83
  140.2 191.3 %all-gather.5.cloned.1.call-start = ((), (), s32[]{:S(2)}) async-start(), calls=%async_computation.8 | async-start | bytes 1730560 | tf_op jit(solution)/shard_map/all_gather | solution.py:78
  159.0 68.8 %copy-start.9 = (bf16[2,1664]{1,0:T(2,128)(2,1)S(1)}, bf16[2,1664]{1,0:T(2,128)(2,1)}, u32[]{:S(2)}) copy-start(bf16[2,1664]{1,0:T(2,128)(2,1)} %param.8) | copy-start | bytes 19972
  221.9 141.7 %all-to-all-start.1 = ((bf16[64,3,6656]{2,1,0:T(4,128)(2,1)}), bf16[64,3,6656]{2,1,0:T(4,128)(2,1)}, u32[]{:S(2)}, u32[]{:S(2)}) async-start(bf16[64,3,6656]{2,1,0:T(4,128)(2,1)} %all_to_all.29), calls=%async_computation.1 | async-start | bytes 6815744 | tf_op jit(solution)/shard_map/all_to_all | solution.py:82
  227.8 107.7 %all-gather.7.cloned.1.call-start = ((), (), s32[]{:S(2)}) async-start(), calls=%async_computation.9 | async-start | bytes 1730560 | tf_op jit(solution)/shard_map/all_gather | solution.py:79
  240.4 184.2 %reduce-scatter.5.cloned.1.call-start = ((), (), s32[]{:S(2)}) async-start(), calls=%async_computation.7 | async-start | bytes 4259840 | tf_op jit(solution)/shard_map/reduce_scatter | solution.py:94
  244.5 87.1 %copy-start.10 = (s32[60]{0:T(128)S(1)}, s32[60]{0:T(128)}, u32[]{:S(2)}) copy-start(s32[60]{0:T(128)} %param.13) | copy-start | bytes 724
  374.3 2.7 copy-start.4
  374.3 2.7 copy-start.5
  377.8 1.2 copy-start.7
  381.3 1.2 copy-start.6
  381.3 88.4 %reduce-scatter.3.cloned.1.call-start = ((), (), s32[]{:S(2)}) async-start(), calls=%async_computation.6 | async-start | bytes 4259840 | tf_op jit(solution)/shard_map/reduce_scatter | solution.py:93
  384.9 0.7 copy-start.11
  389.5 350.2 %copy-start.1 = (bf16[40,6656]{1,0:T(8,128)(2,1)S(1)}, bf16[40,6656]{1,0:T(8,128)(2,1)}, u32[]{:S(2)}) copy-start(bf16[40,6656]{1,0:T(8,128)(2,1)} %param.11) | copy-start | bytes 1597444
Sparse Core Ops, SparseCore 0:
  153.1 84.7 all-gather.4
  240.6 85.1 all-gather.6
  381.5 43.0 reduce-scatter.4
  427.0 42.6 reduce-scatter.2
